TPU v7x, 256 devices: a whole 4x4x8 slice. The times are simulated.
256 devices in a mesh: gx: 16 (over z, x_lo), gy: 16 (over x_hi, y, core).
Axes of the slice: x: 4 (x_hi: 2, x_lo: 2; x = x_hi * 2 + x_lo), y: 4, z: 8, core: 2. Of those that a mesh axis runs over, the one named last changes fastest.
Arguments:
- tokens: bfloat16 [128, 128, 24, 192], P('gx', 'gy'), may hold values from -8 to 8
- cotangent: bfloat16 [128, 128, 24, 192], P('gx', 'gy'), may hold values from -12 to 12
- ln_gain: float32 [192], replicated, may hold values from 0.1 to 1.9
- ln_bias: float32 [192], replicated, may hold values from -3 to 3
- qkv_weight: bfloat16 [192, 576], replicated, may hold values from -1 to 1
- proj_weight: bfloat16 [192, 192], replicated, may hold values from -0.4375 to 0.4375
Outputs:
- block_out: bfloat16 [128, 128, 24, 192], P('gx', 'gy')
- d_tokens: bfloat16 [128, 128, 24, 192], P('gx', 'gy')
- grad_qkv: float32 [192, 576], replicated
- grad_proj: float32 [192, 192], replicated
- grad_gain: float32 [192], replicated
- grad_bias: float32 [192], replicated
All inputs are finite; a program needn't handle non-finite values.
Results may differ from a plain program's by a relative error of at most 0.005.
The roundings to bfloat16 on the way count: a program that leaves them out, or rounds other values in their place, can miss the bound.
Values may be sent and summed in bfloat16 or wider, within the bound.
No kernel may reach another device: no remote copies, remote signals or barrier semaphores. Data moves between devices by JAX's collectives and lax.ppermute only.
A program may use at most 192 MiB of HBM per device.

v0:
```python
import functools
import math

import jax
import jax.numpy as jnp
from jax import lax
from jax.experimental import pallas as pl
from jax.experimental.pallas import tpu as pltpu
from jax.sharding import PartitionSpec as P

HEADS = 12
WIN = 8
SHIFT = 4
F32 = jnp.float32
BF16 = jnp.bfloat16
LOG2E = math.log2(math.e)
MASKED = 2.0**100
LANES = 128
VMEM = pl.BlockSpec(memory_space=pltpu.VMEM)

NT = (((1,), (1,)), ((), ()))
TN = (((0,), (0,)), ((), ()))


def dot(a, b):
    return jnp.dot(a, b, preferred_element_type=F32)


def pieces_of(block):
    channels = block.shape[-1]
    pieces = {}
    for xh in range(2):
        for yh in range(2):
            quad = block[xh * 4 : xh * 4 + 4, yh * 4 : yh * 4 + 4].reshape(16, 24, channels)
            first = quad[:, 4:12].reshape(LANES, channels)
            second = quad[:, 12:20].reshape(LANES, channels)
            pairs = quad.reshape(8, 2, 24, channels)
            high = jnp.concatenate([pairs[:, 0, 20:24], pairs[:, 1, 20:24]], axis=1)
            low = jnp.concatenate([pairs[:, 0, 0:4], pairs[:, 1, 0:4]], axis=1)
            last = jnp.concatenate([high.reshape(64, channels), low.reshape(64, channels)], axis=0)
            pieces[xh, yh] = [piece.T.astype(BF16) for piece in (first, second, last)]
    return pieces


def quadrant_of(first, second, last):
    channels = first.shape[0]
    first = first.astype(F32).T.reshape(16, 8, channels)
    second = second.astype(F32).T.reshape(16, 8, channels)
    last = last.astype(F32).T
    high = last[:64].reshape(8, 8, channels)
    low = last[64:].reshape(8, 8, channels)
    even = jnp.concatenate([low[:, 0:4]], axis=1)
    odd = low[:, 4:8]
    low = jnp.stack([even, odd], axis=1).reshape(16, 4, channels)
    high = jnp.stack([high[:, 0:4], high[:, 4:8]], axis=1).reshape(16, 4, channels)
    whole = jnp.concatenate([low, first, second, high], axis=1)
    return whole.reshape(4, 4, 24, channels).astype(BF16)


def pack_kernel(
    tokens_ref, cot_ref, gain_ref, bias_ref, wqkv_ref, proj_ref,
    *outs,
):
    piece_refs, (gain_out, bias_out, wqkv_t_out, proj_t_out, kf_out, qf_out) = outs[:12], outs[12:]
    for which, ref in enumerate((tokens_ref, cot_ref)):
        pieces = pieces_of(ref[...].astype(F32))
        for xh in range(2):
            for yh in range(2):
                for w in range(3):
                    piece_refs[w * 4 + xh * 2 + yh][which] = pieces[xh, yh][w]
    gain_out[...] = gain_ref[...].T
    bias_out[...] = bias_ref[...].T
    wqkv_t_out[...] = wqkv_ref[...].astype(F32).T.astype(BF16)
    proj_t_out[...] = proj_ref[...].astype(F32).T.astype(BF16)
    edge_x = lax.axis_index("gx") == lax.axis_size("gx") - 1
    edge_y = lax.axis_index("gy") == lax.axis_size("gy") - 1
    shape = kf_out.shape[1:]
    row = lax.broadcasted_iota(jnp.int32, shape, 0)
    lane = lax.broadcasted_iota(jnp.int32, shape, 1)
    for layout, span in enumerate((LANES, LANES // 2)):
        quad = (lane // span) % 4
        far_x = jnp.where(jnp.logical_and(quad // 2 == 0, edge_x), 1.0, 0.0)
        far_y = jnp.where(jnp.logical_and(quad % 2 == 0, edge_y), 1.0, 0.0)
        key = jnp.where(row == 0, far_x, jnp.where(row == 1, 1 - far_x, jnp.where(row == 2, far_y, 1 - far_y)))
        query = jnp.where(row == 0, 1 - far_x, jnp.where(row == 1, far_x, jnp.where(row == 2, 1 - far_y, far_y)))
        kf_out[layout] = jnp.where(row < 4, key, 0.0).astype(BF16)
        qf_out[layout] = jnp.where(row < 4, query * -MASKED, 0.0).astype(BF16)


def packed(tokens, cotangent, gain, bias, wqkv, proj):
    channels = tokens.shape[-1]
    cells = 4 * LANES
    S = jax.ShapeDtypeStruct
    return pl.pallas_call(
        pack_kernel,
        out_shape=(S((2, channels, LANES), BF16),) * 12
        + (
            S((channels, 1), F32),
            S((channels, 1), F32),
            S((3 * channels, channels), BF16),
            S((channels, channels), BF16),
            S((2, 16, cells), BF16),
            S((2, 16, cells), BF16),
        ),
        in_specs=[VMEM] * 6,
        out_specs=(VMEM,) * 18,
        compiler_params=pltpu.CompilerParams(vmem_limit_bytes=40 * 2**20),
        name="pack",
    )(tokens, cotangent, gain[None], bias[None], wqkv, proj)


def unpack_kernel(*refs):
    pieces, outs = refs[:12], refs[12:]
    for which, out in enumerate(outs):
        for xh in range(2):
            for yh in range(2):
                quad = quadrant_of(*(pieces[w * 4 + xh * 2 + yh][which] for w in range(3)))
                out[xh * 4 : xh * 4 + 4, yh * 4 : yh * 4 + 4] = quad


def unpacked(pieces, shape):
    return pl.pallas_call(
        unpack_kernel,
        out_shape=(jax.ShapeDtypeStruct(shape, BF16),) * 2,
        in_specs=[VMEM] * 12,
        out_specs=(VMEM,) * 2,
        compiler_params=pltpu.CompilerParams(vmem_limit_bytes=40 * 2**20),
        name="unpack",
    )(*pieces)


def attend_kernel(
    halves, last,
    q00_ref, q01_ref, q10_ref, q11_ref,
    kf_ref, qf_ref, gain_ref, bias_ref, wqkv_t_ref, wqkv_ref, proj_ref, proj_t_ref, sums_ref,
    y00_ref, y01_ref, y10_ref, y11_ref, grads_ref,
    qkv_s, gm_s, mix_s, gqkv_s,
):
    quads = (q00_ref, q01_ref, q10_ref, q11_ref)
    channels = q00_ref.shape[1]
    hd = channels // HEADS
    cells = 4 * LANES
    half = LANES // 2

    def whole(which):
        if halves:
            parts = [q[which].astype(F32) for q in quads]
            return jnp.concatenate(
                [p[:, :half] for p in parts] + [p[:, half:] for p in parts], axis=1
            )
        return jnp.concatenate([q[which].astype(F32) for q in quads], axis=1)

    xf = whole(0)
    gf = whole(1)
    g = gf.astype(BF16)
    mean = jnp.mean(xf, axis=0, keepdims=True)
    centered = xf - mean
    var = jnp.mean(centered * centered, axis=0, keepdims=True)
    inv = lax.rsqrt(var + 1e-5)
    std = centered * inv
    gain = gain_ref[...]
    normed = (std * gain + bias_ref[...]).astype(BF16)
    qkv_s[...] = dot(wqkv_t_ref[...], normed).astype(BF16)
    gm_s[...] = dot(proj_ref[...], g).astype(BF16)
    size = cells // 2 if halves else cells
    for start in range(0, cells, size):
        cols = slice(start, start + size)
        layout = 1 if halves else 0

        def head(h, carry):
            def rows(base):
                return pl.ds(pl.multiple_of(base + h * hd, hd), hd)

            q = qkv_s[rows(0), cols]
            k = qkv_s[rows(channels), cols]
            v = qkv_s[rows(2 * channels), cols]
            gm = gm_s[rows(0), cols]
            qf = q.astype(F32) * (hd**-0.5 * LOG2E)
            q_hi = qf.astype(BF16)
            q_lo = (qf - q_hi.astype(F32)).astype(BF16)
            ka = jnp.concatenate([k, k, kf_ref[layout, :, cols]], axis=0)
            qa = jnp.concatenate([q_hi, q_lo, qf_ref[layout, :, cols]], axis=0)
            s = lax.dot_general(ka, qa, TN, preferred_element_type=F32)
            e = jnp.exp2(s - jnp.max(s, axis=0, keepdims=True))
            p = e * (1.0 / jnp.sum(e, axis=0, keepdims=True))
            pb = p.astype(BF16)
            o = dot(v, pb)
            mix_s[rows(0), cols] = o.astype(BF16)
            dp = lax.dot_general(v, gm, TN, preferred_element_type=F32)
            inner = jnp.sum(p * dp, axis=0, keepdims=True)
            ds = (p * (dp - inner)).astype(BF16)
            gv = lax.dot_general(gm, pb, NT, preferred_element_type=F32)
            gq = dot(k, ds) * hd**-0.5
            gk = lax.dot_general(q, ds, NT, preferred_element_type=F32) * hd**-0.5
            gqkv_s[rows(0), cols] = gq.astype(BF16)
            gqkv_s[rows(channels), cols] = gk.astype(BF16)
            gqkv_s[rows(2 * channels), cols] = gv.astype(BF16)
            return carry

        lax.fori_loop(0, HEADS, head, 0, unroll=2)
    mixed = mix_s[...]
    block_out = xf + dot(proj_t_ref[...], mixed)
    gqkv = gqkv_s[...]
    gn = dot(wqkv_ref[...], gqkv)
    scaled = gn * gain
    gx = inv * (
        scaled
        - jnp.mean(scaled, axis=0, keepdims=True)
        - std * jnp.mean(scaled * std, axis=0, keepdims=True)
    )
    d_tokens = gf + gx
    for which, y in enumerate((block_out, d_tokens)):
        for i, ref in enumerate((y00_ref, y01_ref, y10_ref, y11_ref)):
            if halves:
                lo = y[:, i * half : (i + 1) * half]
                hi = y[:, cells // 2 + i * half : cells // 2 + (i + 1) * half]
                part = jnp.concatenate([lo, hi], axis=1)
            else:
                part = y[:, i * LANES : (i + 1) * LANES]
            ref[which] = part.astype(BF16)

    dw = lax.dot_general(normed, gqkv, NT, preferred_element_type=F32)
    dproj = lax.dot_general(mixed, g, NT, preferred_element_type=F32)
    dgain = jnp.sum(gn * std, axis=1, keepdims=True)
    dbias = jnp.sum(gn, axis=1, keepdims=True)
    joined = jnp.concatenate([dw, dproj], axis=1)
    blocks = [joined[:, i * LANES : (i + 1) * LANES] for i in range(joined.shape[1] // LANES)]
    lane = lax.broadcasted_iota(jnp.int32, (channels, LANES), 1)
    tail = jnp.where(lane == 0, dgain, jnp.where(lane == 1, dbias, 0.0)).T[:8]
    used = len(blocks) * channels
    grads = jnp.concatenate(blocks, axis=0) + sums_ref[:used]
    extra = jnp.concatenate(
        [tail[:, :LANES], jnp.pad(tail[:, LANES:], ((0, 0), (0, 2 * LANES - channels)))], axis=0
    ) + sums_ref[used : used + 16]
    grads_ref[:used] = grads.astype(grads_ref.dtype)
    grads_ref[used : used + 16] = extra.astype(grads_ref.dtype)
    grads_ref[used + 16 :] = jnp.zeros(
        (grads_ref.shape[0] - used - 16, LANES), grads_ref.dtype
    )


GRAD_ROWS = 1280


def attend(quads, features, gain, bias, wqkv_t, wqkv, proj, proj_t, sums, halves, last):
    channels = quads[0].shape[1]
    cells = 4 * LANES
    S = jax.ShapeDtypeStruct
    return pl.pallas_call(
        functools.partial(attend_kernel, halves, last),
        out_shape=(S((2, channels, LANES), BF16),) * 4
        + (S((GRAD_ROWS, LANES), BF16 if last else F32),),
        in_specs=[VMEM] * 13,
        out_specs=(VMEM,) * 5,
        scratch_shapes=[
            pltpu.VMEM((3 * channels, cells), BF16),
            pltpu.VMEM((channels, cells), BF16),
            pltpu.VMEM((channels, cells), BF16),
            pltpu.VMEM((3 * channels, cells), BF16),
        ],
        compiler_params=pltpu.CompilerParams(vmem_limit_bytes=40 * 2**20),
        cost_estimate=pl.CostEstimate(
            flops=12 * 12 * 512 * 512 * 256, bytes_accessed=4 * 2**20, transcendentals=12 * 512 * 512
        ),
        name="attend",
    )(*quads, *features, gain, bias, wqkv_t, wqkv, proj, proj_t, sums)


def moved(block, step_x, step_y):
    nx, ny = lax.axis_size("gx"), lax.axis_size("gy")
    route = []
    for i in range(nx):
        for j in range(ny):
            to = ((i + step_x) % nx) * ny + (j + step_y) % ny
            route.append((i * ny + j, to))
    return lax.ppermute(block, ("gx", "gy"), route)


def summed(rows):
    nx, ny = lax.axis_size("gx"), lax.axis_size("gy")
    pieces = rows.reshape(ny, -1, LANES)
    got = lax.all_to_all(pieces, "gy", 0, 0)
    mine = jnp.sum(got.astype(F32), axis=0)
    got = lax.all_to_all(jnp.broadcast_to(mine[None], (nx, *mine.shape)), "gx", 0, 0)
    total = jnp.sum(got, axis=0)
    got = lax.all_to_all(jnp.broadcast_to(total[None], (ny, *total.shape)), "gy", 0, 0)
    return got.reshape(rows.shape)


def grads_kernel(factor, rows_ref, dw_ref, dproj_ref, gain_ref, bias_ref):
    channels = dw_ref.shape[0]
    blocks = 4 * channels // LANES
    joined = jnp.concatenate(
        [rows_ref[i * channels : (i + 1) * channels] for i in range(blocks)], axis=1
    ) * factor
    dw_ref[...] = joined[:, : 3 * channels]
    dproj_ref[...] = joined[:, 3 * channels :]
    used = blocks * channels
    tail = rows_ref[used : used + 16] * factor
    tail = jnp.concatenate([tail[:8], tail[8:]], axis=1)[:, :channels]
    gain_ref[...] = tail[0:1]
    bias_ref[...] = tail[1:2]


def grads_of(rows, channels, factor):
    S = jax.ShapeDtypeStruct
    return pl.pallas_call(
        functools.partial(grads_kernel, factor),
        out_shape=(
            S((channels, 3 * channels), F32),
            S((channels, channels), F32),
            S((1, channels), F32),
            S((1, channels), F32),
        ),
        in_specs=[VMEM],
        out_specs=(VMEM,) * 4,
        name="unpack_grads",
    )(rows)


def shards(tokens, cotangent, ln_gain, ln_bias, qkv_weight, proj_weight):
    tile_x, tile_y, depth, channels = tokens.shape
    nx, ny = lax.axis_size("gx"), lax.axis_size("gy")
    windows = depth // WIN
    *pieces, gain, bias, wqkv_t, proj_t, kf, qf = packed(
        tokens, cotangent, ln_gain, ln_bias, qkv_weight, proj_weight
    )
    inputs = []
    for w in range(windows):
        p00, p01, p10, p11 = pieces[w * 4 : w * 4 + 4]
        inputs.append([moved(p00, -1, -1), moved(p01, -1, 0), moved(p10, 0, -1), p11])
    back = []
    sums = jnp.zeros((GRAD_ROWS, LANES), F32)
    for w in range(windows):
        last = w == windows - 1
        if w >= 2:
            inputs[w], back[w - 2] = lax.optimization_barrier((inputs[w], back[w - 2]))
        *ys, sums = attend(
            inputs[w], (kf, qf), gain, bias, wqkv_t, qkv_weight, proj_weight, proj_t, sums,
            halves=last, last=last,
        )
        back.append([moved(ys[0], 1, 1), moved(ys[1], 1, 0), moved(ys[2], 0, 1), ys[3]])
    sums, back[1] = lax.optimization_barrier((sums, back[1]))
    total = summed(sums)
    block_out, d_tokens = unpacked([piece for quads in back for piece in quads], tokens.shape)
    factor = 1.0 / math.sqrt(tile_x * nx * tile_y * ny * depth)
    dw, dproj, dgain, dbias = grads_of(total, channels, factor)
    return block_out, d_tokens, dw, dproj, dgain[0], dbias[0]


def solution(mesh):
    placed = (P("gx", "gy", None, None), P("gx", "gy", None, None), P(), P(), P(), P())
    return jax.shard_map(
        shards,
        mesh=mesh,
        in_specs=placed,
        out_specs=(P("gx", "gy", None, None), P("gx", "gy", None, None), P(), P(), P(), P()),
        check_vma=False,
    )
```

profile of v0, /device:TPU:32, one launch (start us, length us, event | category | flops | bytes accessed | tf_op | source)
XLA Modules:
  0.0 150.9 jit_solution(8253768551796956693)
XLA Ops:
  0.7 0.7 copy-done.7
  1.3 0.0 copy-done.6
  1.3 1.1 copy-done
  2.5 1.1 copy-done.1
  3.6 0.9 copy-done.2
  4.5 0.9 copy-done.4
  5.4 0.7 pack.1
  6.2 4.3 %collective-permute-start.3 = (bf16[2,192,128]{2,1,0:T(8,128)(2,1)S(1)}, bf16[2,192,128]{2,1,0:T(8,128)(2,1)S(1)}, u32[]{:S(2)}, u32[]{:S(2)}) collective-permute-start(bf16[2,192,128]{2,1,0:T(8,128)(2,1)S(1)} %get-tuple-element.62), channel_id=1, source_target_pairs={{0,255},{1,240},{2,241},{3,242},{4,243},{5,244},{6,245},{7,246},{8... | collective-permute-start | bytes 294920 | tf_op jit(solution)/shard_map/ppermute | solution.py:276
  10.4 0.2 collective-permute-start.4
  10.7 2.1 %collective-permute-start.5 = (bf16[2,192,128]{2,1,0:T(8,128)(2,1)S(1)}, bf16[2,192,128]{2,1,0:T(8,128)(2,1)S(1)}, u32[]{:S(2)}, u32[]{:S(2)}) collective-permute-start(bf16[2,192,128]{2,1,0:T(8,128)(2,1)S(1)} %get-tuple-element.64), channel_id=1, source_target_pairs={{0,15},{1,0},{2,1},{3,2},{4,3},{5,4},{6,5},{7,6},{8,7},{9,8},{10,9... | collective-permute-start | bytes 294920 | tf_op jit(solution)/shard_map/ppermute | solution.py:276
  12.7 5.3 %collective-permute-start = (bf16[2,192,128]{2,1,0:T(8,128)(2,1)S(1)}, bf16[2,192,128]{2,1,0:T(8,128)(2,1)S(1)}, u32[]{:S(2)}, u32[]{:S(2)}) collective-permute-start(bf16[2,192,128]{2,1,0:T(8,128)(2,1)S(1)} %get-tuple-element.58), channel_id=1, source_target_pairs={{0,255},{1,240},{2,241},{3,242},{4,243},{5,244},{6,245},{7,246},{8... | collective-permute-start | bytes 294920 | tf_op jit(solution)/shard_map/ppermute | solution.py:276
  18.1 0.6 collective-permute-start.1
  18.7 0.0 collective-permute-done.3.q00_ref
  18.7 1.8 %collective-permute-start.9 = (bf16[2,192,128]{2,1,0:T(8,128)(2,1)S(1)}, bf16[2,192,128]{2,1,0:T(8,128)(2,1)S(1)}, u32[]{:S(2)}, u32[]{:S(2)}) collective-permute-start(bf16[2,192,128]{2,1,0:T(8,128)(2,1)S(1)} %get-tuple-element.84), channel_id=1, source_target_pairs={{0,255},{1,240},{2,241},{3,242},{4,243},{5,244},{6,245},{7,246},{8... | collective-permute-start | bytes 294920 | tf_op jit(solution)/shard_map/ppermute | solution.py:276
  20.4 0.0 collective-permute-done.4.q01_ref
  20.4 0.2 collective-permute-start.10
  20.6 1.9 %collective-permute-start.11 = (bf16[2,192,128]{2,1,0:T(8,128)(2,1)S(1)}, bf16[2,192,128]{2,1,0:T(8,128)(2,1)S(1)}, u32[]{:S(2)}, u32[]{:S(2)}) collective-permute-start(bf16[2,192,128]{2,1,0:T(8,128)(2,1)S(1)} %get-tuple-element.86), channel_id=1, source_target_pairs={{0,15},{1,0},{2,1},{3,2},{4,3},{5,4},{6,5},{7,6},{8,7},{9,8},{10,9... | collective-permute-start | bytes 294920 | tf_op jit(solution)/shard_map/ppermute | solution.py:276
  22.6 0.9 copy-done.3
  23.5 0.1 copy-done.5
  23.5 15.7 %attend.3 = (bf16[2,192,128]{2,1,0:T(8,128)(2,1)S(1)}, bf16[2,192,128]{2,1,0:T(8,128)(2,1)S(1)}, bf16[2,192,128]{2,1,0:T(8,128)(2,1)S(1)}, bf16[2,192,128]{2,1,0:T(8,128)(2,1)S(1)}, f32[1280,128]{1,0:T(8,128)S(1)}) custom-call(bf16[2,192,128]{2,1,0:T(8,128)(2,1)S(1)} %collective-permute-done.3.q00_ref, ...), custom_call_target="tpu_custom_call" | custom-call | flops 9663676416 | bytes 4194304 | tf_op jit(solution)/shard_map/attend/pallas_call | solution.py:249
  39.3 0.0 collective-permute-done.q00_ref
  39.3 0.3 collective-permute-start.2
  39.5 0.0 collective-permute-done.9.q00_ref
  39.5 0.1 collective-permute-start.6
  39.7 0.0 collective-permute-done.10.q01_ref
  39.7 3.1 %collective-permute-start.7 = (bf16[2,192,128]{2,1,0:T(8,128)(2,1)S(1)}, bf16[2,192,128]{2,1,0:T(8,128)(2,1)S(1)}, u32[]{:S(2)}, u32[]{:S(2)}) collective-permute-start(bf16[2,192,128]{2,1,0:T(8,128)(2,1)S(1)} %get-tuple-element.73), channel_id=1, source_target_pairs={{0,16},{1,17},{2,18},{3,19},{4,20},{5,21},{6,22},{7,23},{8,24},{9,... | collective-permute-start | bytes 294920 | tf_op jit(solution)/shard_map/ppermute | solution.py:276
  42.8 0.0 collective-permute-done.11.q10_ref
  42.8 0.0 collective-permute-start.8
  42.8 15.7 %attend.4 = (bf16[2,192,128]{2,1,0:T(8,128)(2,1)S(1)}, bf16[2,192,128]{2,1,0:T(8,128)(2,1)S(1)}, bf16[2,192,128]{2,1,0:T(8,128)(2,1)S(1)}, bf16[2,192,128]{2,1,0:T(8,128)(2,1)S(1)}, f32[1280,128]{1,0:T(8,128)S(1)}) custom-call(bf16[2,192,128]{2,1,0:T(8,128)(2,1)S(1)} %collective-permute-done.9.q00_ref, ...), custom_call_target="tpu_custom_call" | custom-call | flops 9663676416 | bytes 4194304 | tf_op jit(solution)/shard_map/attend/pallas_call | solution.py:249
  58.6 0.0 collective-permute-done.1.q01_ref
  58.6 0.5 collective-permute-start.12
  59.0 0.6 collective-permute-start.13
  59.7 0.5 collective-permute-start.14
  60.2 17.1 %attend.5 = (bf16[2,192,128]{2,1,0:T(8,128)(2,1)S(1)}, bf16[2,192,128]{2,1,0:T(8,128)(2,1)S(1)}, bf16[2,192,128]{2,1,0:T(8,128)(2,1)S(1)}, bf16[2,192,128]{2,1,0:T(8,128)(2,1)S(1)}, bf16[1280,128]{1,0:T(8,128)(2,1)S(1)}) custom-call(bf16[2,192,128]{2,1,0:T(8,128)(2,1)S(1)} %collective-permute-done.q00_ref, ...), custom_call_target="tpu_custom_call" | custom-call | flops 9663676416 | bytes 4194304 | tf_op jit(solution)/shard_map/attend/pallas_call | solution.py:249
  77.3 17.8 %all_to_all.15 = bf16[16,80,128]{2,1,0:T(8,128)(2,1)S(1)} all-to-all(bf16[16,80,128]{2,1,0:T(8,128)(2,1)S(1)} %bitcast.6), channel_id=1, replica_groups=mesh['gx'=16,'gy'=16] {'gy'}, dimensions={0} | all-to-all | bytes 655360 | tf_op jit(solution)/shard_map/all_to_all | solution.py:282
  95.1 0.1 convert_reduce_fusion
  95.2 27.8 %all_to_all.16 = f32[16,80,128]{2,1,0:T(8,128)S(1)} all-to-all(f32[16,80,128]{2,1,0:T(8,128)S(1)} %broadcast_in_dim.24), channel_id=1, replica_groups=mesh['gx'=16,'gy'=16] {'gx'}, dimensions={0} | all-to-all | bytes 1310720 | tf_op jit(solution)/shard_map/all_to_all | solution.py:284
  123.0 0.9 broadcast_in_dim.25
  123.9 4.1 %all-to-all-start.2 = ((f32[16,80,128]{2,1,0:T(8,128)}), f32[16,80,128]{2,1,0:T(8,128)S(1)}, u32[]{:S(2)}, u32[]{:S(2)}) async-start(f32[16,80,128]{2,1,0:T(8,128)} %broadcast_in_dim.25), calls=%async_computation.2 | async-start | bytes 1310720 | tf_op jit(solution)/shard_map/all_to_all | solution.py:286
  128.0 0.2 collective-permute-start.15
  128.2 2.2 %collective-permute-start.16 = (bf16[2,192,128]{2,1,0:T(8,128)(2,1)S(1)}, bf16[2,192,128]{2,1,0:T(8,128)(2,1)S(1)}, u32[]{:S(2)}, u32[]{:S(2)}) collective-permute-start(bf16[2,192,128]{2,1,0:T(8,128)(2,1)S(1)} %get-tuple-element.100), channel_id=1, source_target_pairs={{0,16},{1,17},{2,18},{3,19},{4,20},{5,21},{6,22},{7,23},{8,24},{9,... | collective-permute-start | bytes 294920 | tf_op jit(solution)/shard_map/ppermute | solution.py:276
  130.3 1.2 collective-permute-start.17
  131.5 6.9 %collective-permute-done.15.refs_8_ = bf16[2,192,128]{2,1,0:T(8,128)(2,1)S(1)} collective-permute-done((bf16[2,192,128]{2,1,0:T(8,128)(2,1)S(1)}, bf16[2,192,128]{2,1,0:T(8,128)(2,1)S(1)}, u32[]{:S(2)}, u32[]{:S(2)}) %collective-permute-start.15) | collective-permute-done | bytes 98336 | tf_op jit(solution)/shard_map/ppermute | solution.py:276
  138.4 1.9 %collective-permute-done.16.refs_9_ = bf16[2,192,128]{2,1,0:T(8,128)(2,1)S(1)} collective-permute-done((bf16[2,192,128]{2,1,0:T(8,128)(2,1)S(1)}, bf16[2,192,128]{2,1,0:T(8,128)(2,1)S(1)}, u32[]{:S(2)}, u32[]{:S(2)}) %collective-permute-start.16) | collective-permute-done | bytes 98336 | tf_op jit(solution)/shard_map/ppermute | solution.py:276
  140.3 6.1 %collective-permute-done.17.refs_10_ = bf16[2,192,128]{2,1,0:T(8,128)(2,1)S(1)} collective-permute-done((bf16[2,192,128]{2,1,0:T(8,128)(2,1)S(1)}, bf16[2,192,128]{2,1,0:T(8,128)(2,1)S(1)}, u32[]{:S(2)}, u32[]{:S(2)}) %collective-permute-start.17) | collective-permute-done | bytes 98336 | tf_op jit(solution)/shard_map/ppermute | solution.py:276
  146.5 1.6 %unpack.1 = (bf16[8,8,24,192]{3,2,1,0:T(8,128)(2,1)}, bf16[8,8,24,192]{3,2,1,0:T(8,128)(2,1)}) custom-call(bf16[2,192,128]{2,1,0:T(8,128)(2,1)S(1)} %collective-permute-done.6.refs_0_, bf16[2,192,128]{2,1,0:T(8,128)(2,1)S(1)} %collective-permute-done.7.refs_1_, bf16[2,192,128]{2,1,0:T(8,128)(2,1)S(1)} %collective-permute-done.8.refs_2_, ...), custom_call_target="tpu_custom_call" | custom-call | tf_op jit(solution)/shard_map/unpack/pallas_call | solution.py:122
  148.1 0.8 copy-done.8
  148.9 2.0 %unpack_grads.1 = (f32[192,576]{1,0:T(8,128)}, f32[192,192]{1,0:T(8,128)}, f32[1,192]{1,0:T(1,128)}, f32[1,192]{1,0:T(1,128)}) custom-call(f32[1280,128]{1,0:T(8,128)} %bitcast.9), custom_call_target="tpu_custom_call" | custom-call | tf_op jit(solution)/shard_map/unpack_grads/pallas_call | solution.py:307
  (21 shorter events, 0.2 us)
Async XLA Ops:
  0.6 0.7 copy-start.7
  0.6 0.7 copy-start.6
  1.3 1.1 copy-start
  2.5 1.1 copy-start.1
  3.6 0.9 copy-start.2
  4.5 0.9 copy-start.4
  6.2 12.5 %collective-permute-start.3 = (bf16[2,192,128]{2,1,0:T(8,128)(2,1)S(1)}, bf16[2,192,128]{2,1,0:T(8,128)(2,1)S(1)}, u32[]{:S(2)}, u32[]{:S(2)}) collective-permute-start(bf16[2,192,128]{2,1,0:T(8,128)(2,1)S(1)} %get-tuple-element.62), channel_id=1, source_target_pairs={{0,255},{1,240},{2,241},{3,242},{4,243},{5,244},{6,245},{7,246},{8... | collective-permute-start | bytes 294920 | tf_op jit(solution)/shard_map/ppermute | solution.py:276
  10.4 10.0 %collective-permute-start.4 = (bf16[2,192,128]{2,1,0:T(8,128)(2,1)S(1)}, bf16[2,192,128]{2,1,0:T(8,128)(2,1)S(1)}, u32[]{:S(2)}, u32[]{:S(2)}) collective-permute-start(bf16[2,192,128]{2,1,0:T(8,128)(2,1)S(1)} %get-tuple-element.63), channel_id=1, source_target_pairs={{0,240},{1,241},{2,242},{3,243},{4,244},{5,245},{6,246},{7,247},{8... | collective-permute-start | bytes 294920 | tf_op jit(solution)/shard_map/ppermute | solution.py:276
  10.7 10.0 %collective-permute-start.5 = (bf16[2,192,128]{2,1,0:T(8,128)(2,1)S(1)}, bf16[2,192,128]{2,1,0:T(8,128)(2,1)S(1)}, u32[]{:S(2)}, u32[]{:S(2)}) collective-permute-start(bf16[2,192,128]{2,1,0:T(8,128)(2,1)S(1)} %get-tuple-element.64), channel_id=1, source_target_pairs={{0,15},{1,0},{2,1},{3,2},{4,3},{5,4},{6,5},{7,6},{8,7},{9,8},{10,9... | collective-permute-start | bytes 294920 | tf_op jit(solution)/shard_map/ppermute | solution.py:276
  12.7 26.5 %collective-permute-start = (bf16[2,192,128]{2,1,0:T(8,128)(2,1)S(1)}, bf16[2,192,128]{2,1,0:T(8,128)(2,1)S(1)}, u32[]{:S(2)}, u32[]{:S(2)}) collective-permute-start(bf16[2,192,128]{2,1,0:T(8,128)(2,1)S(1)} %get-tuple-element.58), channel_id=1, source_target_pairs={{0,255},{1,240},{2,241},{3,242},{4,243},{5,244},{6,245},{7,246},{8... | collective-permute-start | bytes 294920 | tf_op jit(solution)/shard_map/ppermute | solution.py:276
  18.1 40.5 %collective-permute-start.1 = (bf16[2,192,128]{2,1,0:T(8,128)(2,1)S(1)}, bf16[2,192,128]{2,1,0:T(8,128)(2,1)S(1)}, u32[]{:S(2)}, u32[]{:S(2)}) collective-permute-start(bf16[2,192,128]{2,1,0:T(8,128)(2,1)S(1)} %get-tuple-element.59), channel_id=1, source_target_pairs={{0,240},{1,241},{2,242},{3,243},{4,244},{5,245},{6,246},{7,247},{8... | collective-permute-start | bytes 294920 | tf_op jit(solution)/shard_map/ppermute | solution.py:276
  18.7 20.9 %collective-permute-start.9 = (bf16[2,192,128]{2,1,0:T(8,128)(2,1)S(1)}, bf16[2,192,128]{2,1,0:T(8,128)(2,1)S(1)}, u32[]{:S(2)}, u32[]{:S(2)}) collective-permute-start(bf16[2,192,128]{2,1,0:T(8,128)(2,1)S(1)} %get-tuple-element.84), channel_id=1, source_target_pairs={{0,255},{1,240},{2,241},{3,242},{4,243},{5,244},{6,245},{7,246},{8... | collective-permute-start | bytes 294920 | tf_op jit(solution)/shard_map/ppermute | solution.py:276
  20.4 19.3 %collective-permute-start.10 = (bf16[2,192,128]{2,1,0:T(8,128)(2,1)S(1)}, bf16[2,192,128]{2,1,0:T(8,128)(2,1)S(1)}, u32[]{:S(2)}, u32[]{:S(2)}) collective-permute-start(bf16[2,192,128]{2,1,0:T(8,128)(2,1)S(1)} %get-tuple-element.85), channel_id=1, source_target_pairs={{0,240},{1,241},{2,242},{3,243},{4,244},{5,245},{6,246},{7,247},{8... | collective-permute-start | bytes 294920 | tf_op jit(solution)/shard_map/ppermute | solution.py:276
  20.6 22.2 %collective-permute-start.11 = (bf16[2,192,128]{2,1,0:T(8,128)(2,1)S(1)}, bf16[2,192,128]{2,1,0:T(8,128)(2,1)S(1)}, u32[]{:S(2)}, u32[]{:S(2)}) collective-permute-start(bf16[2,192,128]{2,1,0:T(8,128)(2,1)S(1)} %get-tuple-element.86), channel_id=1, source_target_pairs={{0,15},{1,0},{2,1},{3,2},{4,3},{5,4},{6,5},{7,6},{8,7},{9,8},{10,9... | collective-permute-start | bytes 294920 | tf_op jit(solution)/shard_map/ppermute | solution.py:276
  22.5 0.9 copy-start.3
  22.5 1.0 copy-start.5
  39.3 19.8 %collective-permute-start.2 = (bf16[2,192,128]{2,1,0:T(8,128)(2,1)S(1)}, bf16[2,192,128]{2,1,0:T(8,128)(2,1)S(1)}, u32[]{:S(2)}, u32[]{:S(2)}) collective-permute-start(bf16[2,192,128]{2,1,0:T(8,128)(2,1)S(1)} %get-tuple-element.60), channel_id=1, source_target_pairs={{0,15},{1,0},{2,1},{3,2},{4,3},{5,4},{6,5},{7,6},{8,7},{9,8},{10,9... | collective-permute-start | bytes 294920 | tf_op jit(solution)/shard_map/ppermute | solution.py:276
  39.5 20.1 %collective-permute-start.6 = (bf16[2,192,128]{2,1,0:T(8,128)(2,1)S(1)}, bf16[2,192,128]{2,1,0:T(8,128)(2,1)S(1)}, u32[]{:S(2)}, u32[]{:S(2)}) collective-permute-start(bf16[2,192,128]{2,1,0:T(8,128)(2,1)S(1)} %get-tuple-element.72), channel_id=1, source_target_pairs={{0,17},{1,18},{2,19},{3,20},{4,21},{5,22},{6,23},{7,24},{8,25},{9,... | collective-permute-start | bytes 294920 | tf_op jit(solution)/shard_map/ppermute | solution.py:276
  39.7 20.5 %collective-permute-start.7 = (bf16[2,192,128]{2,1,0:T(8,128)(2,1)S(1)}, bf16[2,192,128]{2,1,0:T(8,128)(2,1)S(1)}, u32[]{:S(2)}, u32[]{:S(2)}) collective-permute-start(bf16[2,192,128]{2,1,0:T(8,128)(2,1)S(1)} %get-tuple-element.73), channel_id=1, source_target_pairs={{0,16},{1,17},{2,18},{3,19},{4,20},{5,21},{6,22},{7,23},{8,24},{9,... | collective-permute-start | bytes 294920 | tf_op jit(solution)/shard_map/ppermute | solution.py:276
  42.8 17.4 %collective-permute-start.8 = (bf16[2,192,128]{2,1,0:T(8,128)(2,1)S(1)}, bf16[2,192,128]{2,1,0:T(8,128)(2,1)S(1)}, u32[]{:S(2)}, u32[]{:S(2)}) collective-permute-start(bf16[2,192,128]{2,1,0:T(8,128)(2,1)S(1)} %get-tuple-element.74), channel_id=1, source_target_pairs={{0,1},{1,2},{2,3},{3,4},{4,5},{5,6},{6,7},{7,8},{8,9},{9,10},{10,1... | collective-permute-start | bytes 294920 | tf_op jit(solution)/shard_map/ppermute | solution.py:276
  58.6 18.7 %collective-permute-start.12 = (bf16[2,192,128]{2,1,0:T(8,128)(2,1)S(1)}, bf16[2,192,128]{2,1,0:T(8,128)(2,1)S(1)}, u32[]{:S(2)}, u32[]{:S(2)}) collective-permute-start(bf16[2,192,128]{2,1,0:T(8,128)(2,1)S(1)} %get-tuple-element.91), channel_id=1, source_target_pairs={{0,17},{1,18},{2,19},{3,20},{4,21},{5,22},{6,23},{7,24},{8,25},{9,... | collective-permute-start | bytes 294920 | tf_op jit(solution)/shard_map/ppermute | solution.py:276
  59.0 18.2 %collective-permute-start.13 = (bf16[2,192,128]{2,1,0:T(8,128)(2,1)S(1)}, bf16[2,192,128]{2,1,0:T(8,128)(2,1)S(1)}, u32[]{:S(2)}, u32[]{:S(2)}) collective-permute-start(bf16[2,192,128]{2,1,0:T(8,128)(2,1)S(1)} %get-tuple-element.92), channel_id=1, source_target_pairs={{0,16},{1,17},{2,18},{3,19},{4,20},{5,21},{6,22},{7,23},{8,24},{9,... | collective-permute-start | bytes 294920 | tf_op jit(solution)/shard_map/ppermute | solution.py:276
  59.7 17.6 %collective-permute-start.14 = (bf16[2,192,128]{2,1,0:T(8,128)(2,1)S(1)}, bf16[2,192,128]{2,1,0:T(8,128)(2,1)S(1)}, u32[]{:S(2)}, u32[]{:S(2)}) collective-permute-start(bf16[2,192,128]{2,1,0:T(8,128)(2,1)S(1)} %get-tuple-element.93), channel_id=1, source_target_pairs={{0,1},{1,2},{2,3},{3,4},{4,5},{5,6},{6,7},{7,8},{8,9},{9,10},{10,1... | collective-permute-start | bytes 294920 | tf_op jit(solution)/shard_map/ppermute | solution.py:276
  123.9 24.2 %all-to-all-start.2 = ((f32[16,80,128]{2,1,0:T(8,128)}), f32[16,80,128]{2,1,0:T(8,128)S(1)}, u32[]{:S(2)}, u32[]{:S(2)}) async-start(f32[16,80,128]{2,1,0:T(8,128)} %broadcast_in_dim.25), calls=%async_computation.2 | async-start | bytes 1310720 | tf_op jit(solution)/shard_map/all_to_all | solution.py:286
  128.0 10.4 %collective-permute-start.15 = (bf16[2,192,128]{2,1,0:T(8,128)(2,1)S(1)}, bf16[2,192,128]{2,1,0:T(8,128)(2,1)S(1)}, u32[]{:S(2)}, u32[]{:S(2)}) collective-permute-start(bf16[2,192,128]{2,1,0:T(8,128)(2,1)S(1)} %get-tuple-element.99), channel_id=1, source_target_pairs={{0,17},{1,18},{2,19},{3,20},{4,21},{5,22},{6,23},{7,24},{8,25},{9,... | collective-permute-start | bytes 294920 | tf_op jit(solution)/shard_map/ppermute | solution.py:276
  128.2 12.2 %collective-permute-start.16 = (bf16[2,192,128]{2,1,0:T(8,128)(2,1)S(1)}, bf16[2,192,128]{2,1,0:T(8,128)(2,1)S(1)}, u32[]{:S(2)}, u32[]{:S(2)}) collective-permute-start(bf16[2,192,128]{2,1,0:T(8,128)(2,1)S(1)} %get-tuple-element.100), channel_id=1, source_target_pairs={{0,16},{1,17},{2,18},{3,19},{4,20},{5,21},{6,22},{7,23},{8,24},{9,... | collective-permute-start | bytes 294920 | tf_op jit(solution)/shard_map/ppermute | solution.py:276
  130.3 16.2 %collective-permute-start.17 = (bf16[2,192,128]{2,1,0:T(8,128)(2,1)S(1)}, bf16[2,192,128]{2,1,0:T(8,128)(2,1)S(1)}, u32[]{:S(2)}, u32[]{:S(2)}) collective-permute-start(bf16[2,192,128]{2,1,0:T(8,128)(2,1)S(1)} %get-tuple-element.101), channel_id=1, source_target_pairs={{0,1},{1,2},{2,3},{3,4},{4,5},{5,6},{6,7},{7,8},{8,9},{9,10},{10,1... | collective-permute-start | bytes 294920 | tf_op jit(solution)/shard_map/ppermute | solution.py:276
  148.1 0.8 copy-start.8
where the time goes:
time: 151 us
  Pallas kernels  52.8 us (35%)
  blocking collectives  45.6 us (30%)
  starting transfers between devices  29.1 us (19%)
  waiting for transfers between devices  15 us (10%)
  local copies, waits for them, and re-layouts  7.55 us (5%)
    pallas_call x3, Pallas kernels, attend(): pl.pallas_call(functools.partial(attend_kernel, halves, last), out_shape=...  48.5 us
    all_to_all x1, blocking collectives, summed(): lax.all_to_all(jnp.broadcast_to(mine[None], (nx, *mine.shape)), 'gx', 0, 0)  27.8 us
    ppermute x18, starting transfers between devices, moved(): return lax.ppermute(block, ('gx', 'gy'), route)  25 us
    all_to_all x1, blocking collectives, summed(): got = lax.all_to_all(pieces, 'gy', 0, 0)  17.8 us
    ppermute x18, waiting for transfers between devices, moved(): return lax.ppermute(block, ('gx', 'gy'), route)  15 us
    unnamed x18, local copies, waits for them, and re-layouts  6.58 us
    all_to_all x1, starting transfers between devices, summed(): lax.all_to_all(jnp.broadcast_to(total[None], (ny, *total.shape)), 'gy', 0...  4.07 us
  transfers between devices with their start and end apart: 19, of which 3 were waited for; matrix products, arithmetic and copies ran while one was open for 0% of the time, Pallas kernels for 33%

commit v1 on v0

--- a/solution.py
+++ b/solution.py
@@ -134,7 +134,7 @@
     q00_ref, q01_ref, q10_ref, q11_ref,
     kf_ref, qf_ref, gain_ref, bias_ref, wqkv_t_ref, wqkv_ref, proj_ref, proj_t_ref, sums_ref,
     y00_ref, y01_ref, y10_ref, y11_ref, grads_ref,
-    qkv_s, gm_s, mix_s, gqkv_s,
+    qkv_s, gm_s, mix_s, gqkv_s, kv_s, qa_s, ga_s, e_s, pb_s, dp_s, ds_s, r_s, d_s,
 ):
     quads = (q00_ref, q01_ref, q10_ref, q11_ref)
     channels = q00_ref.shape[1]
@@ -160,44 +160,167 @@
     std = centered * inv
     gain = gain_ref[...]
     normed = (std * gain + bias_ref[...]).astype(BF16)
-    qkv_s[...] = dot(wqkv_t_ref[...], normed).astype(BF16)
+    qkv = dot(wqkv_t_ref[...], normed).astype(BF16)
+    qkv_s[...] = qkv
     gm_s[...] = dot(proj_ref[...], g).astype(BF16)
+
+    layout = 1 if halves else 0
     size = cells // 2 if halves else cells
-    for start in range(0, cells, size):
-        cols = slice(start, start + size)
-        layout = 1 if halves else 0
-
+    groups = [slice(start, start + size) for start in range(0, cells, size)]
+    step_rows = 64 * (cells // size)
+    chunks = [
+        (gi, slice(c, c + step_rows), group)
+        for gi, group in enumerate(groups)
+        for c in range(group.start, group.stop, step_rows)
+    ]
+    scale = hd**-0.5
+
+    def head_rows(base, h):
+        if isinstance(h, int):
+            return slice(base + h * hd, base + (h + 1) * hd)
+        return pl.ds(pl.multiple_of(base + h * hd, hd), hd)
+
+    def q_rows(h):
+        return head_rows(0, h)
+
+    def k_rows(h):
+        return head_rows(channels, h)
+
+    def v_rows(h):
+        return head_rows(2 * channels, h)
+
+    def folded(x):
+        return jnp.sum(x.reshape(-1, 8, x.shape[-1]), axis=0)
+
+    def added(total, gi, x):
+        total[gi] = x if total[gi] is None else total[gi] + x
+
+    def prepare(h, slot):
+        k = qkv_s[k_rows(h)]
+        qf = qkv_s[q_rows(h)].astype(F32) * (scale * LOG2E)
+        q_hi = qf.astype(BF16)
+        q_lo = (qf - q_hi.astype(F32)).astype(BF16)
+        none = jnp.zeros_like(k)
+        kv_s[slot] = jnp.concatenate([k, k, kf_ref[layout], qkv_s[v_rows(h)]], axis=0).T
+        qa_s[slot] = jnp.concatenate([q_hi, q_lo, qf_ref[layout], none], axis=0)
+        ga_s[slot] = jnp.concatenate([none, none, none, gm_s[q_rows(h)]], axis=0)
+
+    def exponentials(slot, chunk, total):
+        gi, rows, cols = chunk
+        e = jnp.exp2(dot(kv_s[slot, rows], qa_s[slot, :, cols]))
+        e_s[slot, rows] = e
+        added(total, gi, folded(e))
+
+    def attention(slot, chunk, total):
+        gi, rows, cols = chunk
+        p = e_s[slot, rows] * r_s[slot, 0:1, cols]
+        e_s[slot, rows] = p
+        pb_s[rows] = p.astype(BF16)
+        dp = dot(kv_s[slot, rows], ga_s[slot, :, cols])
+        dp_s[rows] = dp
+        added(total, gi, folded(p * dp))
+
+    def grad_scores(slot, chunk):
+        _, rows, cols = chunk
+        ds_s[slot, rows] = (e_s[slot, rows] * (dp_s[rows] - d_s[0:1, cols])).astype(BF16)
+
+    def mixed_of(h):
+        for cols in groups:
+            mix_s[q_rows(h), cols] = dot(qkv_s[v_rows(h), cols], pb_s[cols]).astype(BF16)
+
+    def grad_values_of(h):
+        for cols in groups:
+            gv = lax.dot_general(gm_s[q_rows(h), cols], pb_s[cols], NT, preferred_element_type=F32)
+            gqkv_s[v_rows(h), cols] = gv.astype(BF16)
+
+    def grad_queries_of(h, slot):
+        for cols in groups:
+            gq = dot(qkv_s[k_rows(h), cols], ds_s[slot, cols]) * scale
+            gqkv_s[q_rows(h), cols] = gq.astype(BF16)
+
+    def grad_keys_of(h, slot):
+        for cols in groups:
+            gk = lax.dot_general(
+                qkv_s[q_rows(h), cols], ds_s[slot, cols], NT, preferred_element_type=F32
+            )
+            gqkv_s[k_rows(h), cols] = (gk * scale).astype(BF16)
+
+    def keep_inverse(slot, total):
+        for gi, cols in enumerate(groups):
+            r_s[slot, 0:1, cols] = 1.0 / jnp.sum(total[gi], axis=0, keepdims=True)
+
+    def step(i, slot, first=True, final=True, ahead=True):
+        sums = [None] * len(groups)
+        inner = [None] * len(groups)
+        count = len(chunks)
+        for c, chunk in enumerate(chunks):
+            if first:
+                exponentials(slot, chunk, sums)
+            attention(1 - slot, chunk, inner)
+            if final and c == count // 4:
+                grad_queries_of(i - 2, slot)
+            if final and c == 3 * count // 4:
+                grad_keys_of(i - 2, slot)
+        if first:
+            keep_inverse(slot, sums)
+        for gi, cols in enumerate(groups):
+            d_s[0:1, cols] = jnp.sum(inner[gi], axis=0, keepdims=True)
+        for c, chunk in enumerate(chunks):
+            grad_scores(1 - slot, chunk)
+            if c == 0:
+                mixed_of(i - 1)
+            if c == count // 2:
+                grad_values_of(i - 1)
+        if ahead:
+            prepare(i + 1, 1 - slot)
+
+    squares = jnp.square(qkv[: 2 * channels].astype(F32)).reshape(2 * HEADS, hd, cells)
+    longest = jnp.max(jnp.sum(squares, axis=1), axis=1, keepdims=True)
+    bound = jnp.max(longest[:HEADS] * longest[HEADS:]) * (scale * LOG2E) ** 2
+    in_range = bound <= 110.0**2
+
+    @pl.when(in_range)
+    def _():
+        prepare(0, 0)
+        prepare(1, 1)
+        sums = [None] * len(groups)
+        for chunk in chunks:
+            exponentials(0, chunk, sums)
+        keep_inverse(0, sums)
+        step(1, 1, final=False)
+
+        def two_steps(j, carry):
+            step(2 + 2 * j, 0)
+            step(3 + 2 * j, 1)
+            return carry
+
+        lax.fori_loop(0, (HEADS - 4) // 2, two_steps, 0)
+        step(HEADS - 2, 0)
+        step(HEADS - 1, 1, ahead=False)
+        step(HEADS, 0, first=False, ahead=False)
+        grad_queries_of(HEADS - 1, 1)
+        grad_keys_of(HEADS - 1, 1)
+
+    @pl.when(jnp.logical_not(in_range))
+    def _():
         def head(h, carry):
-            def rows(base):
-                return pl.ds(pl.multiple_of(base + h * hd, hd), hd)
-
-            q = qkv_s[rows(0), cols]
-            k = qkv_s[rows(channels), cols]
-            v = qkv_s[rows(2 * channels), cols]
-            gm = gm_s[rows(0), cols]
-            qf = q.astype(F32) * (hd**-0.5 * LOG2E)
-            q_hi = qf.astype(BF16)
-            q_lo = (qf - q_hi.astype(F32)).astype(BF16)
-            ka = jnp.concatenate([k, k, kf_ref[layout, :, cols]], axis=0)
-            qa = jnp.concatenate([q_hi, q_lo, qf_ref[layout, :, cols]], axis=0)
-            s = lax.dot_general(ka, qa, TN, preferred_element_type=F32)
-            e = jnp.exp2(s - jnp.max(s, axis=0, keepdims=True))
-            p = e * (1.0 / jnp.sum(e, axis=0, keepdims=True))
-            pb = p.astype(BF16)
-            o = dot(v, pb)
-            mix_s[rows(0), cols] = o.astype(BF16)
-            dp = lax.dot_general(v, gm, TN, preferred_element_type=F32)
-            inner = jnp.sum(p * dp, axis=0, keepdims=True)
-            ds = (p * (dp - inner)).astype(BF16)
-            gv = lax.dot_general(gm, pb, NT, preferred_element_type=F32)
-            gq = dot(k, ds) * hd**-0.5
-            gk = lax.dot_general(q, ds, NT, preferred_element_type=F32) * hd**-0.5
-            gqkv_s[rows(0), cols] = gq.astype(BF16)
-            gqkv_s[rows(channels), cols] = gk.astype(BF16)
-            gqkv_s[rows(2 * channels), cols] = gv.astype(BF16)
+            prepare(h, 0)
+            for cols in groups:
+                s = dot(kv_s[0, cols], qa_s[0, :, cols])
+                e = jnp.exp2(s - jnp.max(s, axis=0, keepdims=True))
+                p = e * (1.0 / jnp.sum(e, axis=0, keepdims=True))
+                pb_s[cols] = p.astype(BF16)
+                dp = dot(kv_s[0, cols], ga_s[0, :, cols])
+                inner = jnp.sum(p * dp, axis=0, keepdims=True)
+                ds_s[0, cols] = (p * (dp - inner)).astype(BF16)
+            mixed_of(h)
+            grad_values_of(h)
+            grad_queries_of(h, 0)
+            grad_keys_of(h, 0)
             return carry
 
-        lax.fori_loop(0, HEADS, head, 0, unroll=2)
+        lax.fori_loop(0, HEADS, head, 0)
+
     mixed = mix_s[...]
     block_out = xf + dot(proj_t_ref[...], mixed)
     gqkv = gqkv_s[...]
@@ -245,6 +368,7 @@
 def attend(quads, features, gain, bias, wqkv_t, wqkv, proj, proj_t, sums, halves, last):
     channels = quads[0].shape[1]
     cells = 4 * LANES
+    width = cells // 2 if halves else cells
     S = jax.ShapeDtypeStruct
     return pl.pallas_call(
         functools.partial(attend_kernel, halves, last),
@@ -257,6 +381,15 @@
             pltpu.VMEM((channels, cells), BF16),
             pltpu.VMEM((channels, cells), BF16),
             pltpu.VMEM((3 * channels, cells), BF16),
+            pltpu.VMEM((2, cells, 64), BF16),
+            pltpu.VMEM((2, 64, cells), BF16),
+            pltpu.VMEM((2, 64, cells), BF16),
+            pltpu.VMEM((2, cells, width), F32),
+            pltpu.VMEM((cells, width), BF16),
+            pltpu.VMEM((cells, width), F32),
+            pltpu.VMEM((2, cells, width), BF16),
+            pltpu.VMEM((2, 8, cells), F32),
+            pltpu.VMEM((8, cells), F32),
         ],
         compiler_params=pltpu.CompilerParams(vmem_limit_bytes=40 * 2**20),
         cost_estimate=pl.CostEstimate(
@@ -276,27 +409,36 @@
     return lax.ppermute(block, ("gx", "gy"), route)
 
 
-def summed(rows):
+def summed(rows, beside):
     nx, ny = lax.axis_size("gx"), lax.axis_size("gy")
-    pieces = rows.reshape(ny, -1, LANES)
-    got = lax.all_to_all(pieces, "gy", 0, 0)
-    mine = jnp.sum(got.astype(F32), axis=0)
-    got = lax.all_to_all(jnp.broadcast_to(mine[None], (nx, *mine.shape)), "gx", 0, 0)
-    total = jnp.sum(got, axis=0)
-    got = lax.all_to_all(jnp.broadcast_to(total[None], (ny, *total.shape)), "gy", 0, 0)
-    return got.reshape(rows.shape)
+    near = 2 * ny
+    planes = [[near * i + j for j in range(near)] for i in range(nx // 2)]
+    across = [list(ids) for ids in zip(*planes)]
+
+    def exchanged(pieces, groups):
+        return lax.all_to_all(pieces, ("gx", "gy"), 0, 0, axis_index_groups=groups)
+
+    def copies(piece, count):
+        return jnp.broadcast_to(piece[None], (count, *piece.shape))
+
+    got = exchanged(rows.reshape(near, -1, LANES), planes)
+    got, beside = lax.optimization_barrier((got, beside))
+    mine = jnp.sum(got.astype(F32), axis=0).astype(BF16)
+    got = exchanged(copies(mine, nx // 2), across)
+    total = jnp.sum(got.astype(F32), axis=0).astype(BF16)
+    return exchanged(copies(total, near), planes).reshape(rows.shape), beside
 
 
 def grads_kernel(factor, rows_ref, dw_ref, dproj_ref, gain_ref, bias_ref):
     channels = dw_ref.shape[0]
     blocks = 4 * channels // LANES
     joined = jnp.concatenate(
-        [rows_ref[i * channels : (i + 1) * channels] for i in range(blocks)], axis=1
+        [rows_ref[i * channels : (i + 1) * channels].astype(F32) for i in range(blocks)], axis=1
     ) * factor
     dw_ref[...] = joined[:, : 3 * channels]
     dproj_ref[...] = joined[:, 3 * channels :]
     used = blocks * channels
-    tail = rows_ref[used : used + 16] * factor
+    tail = rows_ref[used : used + 16].astype(F32) * factor
     tail = jnp.concatenate([tail[:8], tail[8:]], axis=1)[:, :channels]
     gain_ref[...] = tail[0:1]
     bias_ref[...] = tail[1:2]
@@ -341,7 +483,7 @@
         )
         back.append([moved(ys[0], 1, 1), moved(ys[1], 1, 0), moved(ys[2], 0, 1), ys[3]])
     sums, back[1] = lax.optimization_barrier((sums, back[1]))
-    total = summed(sums)
+    total, back = summed(sums, back)
     block_out, d_tokens = unpacked([piece for quads in back for piece in quads], tokens.shape)
     factor = 1.0 / math.sqrt(tile_x * nx * tile_y * ny * depth)
     dw, dproj, dgain, dbias = grads_of(total, channels, factor)

time: 151 us -> 131 us (0.87)
  the two profiles are of different devices: /device:TPU:32 before, /device:TPU:1 now
where the time goes in v1:
time: 131 us; the launch traced here: 130 us
  starting transfers between devices  49 us (37%)
  Pallas kernels  40 us (31%)
  blocking collectives  16.3 us (12%)
  waiting for transfers between devices  16.1 us (12%)
  local copies, waits for them, and re-layouts  7.3 us (6%)
    ppermute x18, starting transfers between devices, moved(): return lax.ppermute(block, ('gx', 'gy'), route)  36.4 us
    pallas_call x3, Pallas kernels, attend(): pl.pallas_call(functools.partial(attend_kernel, halves, last), out_shape=...  35.7 us
    all_to_all x1, blocking collectives, exchanged(): return lax.all_to_all(pieces, ('gx', 'gy'), 0, 0, axis_index_groups=groups)  16.3 us
    all_to_all x2, starting transfers between devices, exchanged(): return lax.all_to_all(pieces, ('gx', 'gy'), 0, 0, axis_index_groups=groups)  12.7 us
    all_to_all x2, waiting for transfers between devices, exchanged(): return lax.all_to_all(pieces, ('gx', 'gy'), 0, 0, axis_index_groups=groups)  8.2 us
    ppermute x18, waiting for transfers between devices, moved(): return lax.ppermute(block, ('gx', 'gy'), route)  7.94 us
    unnamed x18, local copies, waits for them, and re-layouts  6.47 us
  transfers between devices with their start and end apart: 20, of which 3 were waited for; matrix products, arithmetic and copies ran while one was open for 0% of the time, Pallas kernels for 29%

profile of v1, /device:TPU:1, one launch (start us, length us, event | category | flops | bytes accessed | tf_op | source)
XLA Modules:
  0.0 129.6 jit_solution(376980218458038053)
XLA Ops:
  0.7 0.7 copy-done.7
  1.3 0.0 copy-done.6
  1.3 1.1 copy-done
  2.5 1.1 copy-done.1
  3.6 0.9 copy-done.2
  4.5 0.9 copy-done.4
  5.4 0.7 pack.1
  6.2 8.0 %collective-permute-start.3 = (bf16[2,192,128]{2,1,0:T(8,128)(2,1)S(1)}, bf16[2,192,128]{2,1,0:T(8,128)(2,1)S(1)}, u32[]{:S(2)}, u32[]{:S(2)}) collective-permute-start(bf16[2,192,128]{2,1,0:T(8,128)(2,1)S(1)} %get-tuple-element.75), channel_id=1, source_target_pairs={{0,255},{1,240},{2,241},{3,242},{4,243},{5,244},{6,245},{7,246},{8... | collective-permute-start | bytes 294920 | tf_op jit(solution)/shard_map/ppermute | solution.py:409
  14.1 0.3 collective-permute-start.4
  14.4 3.5 %collective-permute-start.5 = (bf16[2,192,128]{2,1,0:T(8,128)(2,1)S(1)}, bf16[2,192,128]{2,1,0:T(8,128)(2,1)S(1)}, u32[]{:S(2)}, u32[]{:S(2)}) collective-permute-start(bf16[2,192,128]{2,1,0:T(8,128)(2,1)S(1)} %get-tuple-element.77), channel_id=1, source_target_pairs={{0,15},{1,0},{2,1},{3,2},{4,3},{5,4},{6,5},{7,6},{8,7},{9,8},{10,9... | collective-permute-start | bytes 294920 | tf_op jit(solution)/shard_map/ppermute | solution.py:409
  17.9 2.7 %collective-permute-start = (bf16[2,192,128]{2,1,0:T(8,128)(2,1)S(1)}, bf16[2,192,128]{2,1,0:T(8,128)(2,1)S(1)}, u32[]{:S(2)}, u32[]{:S(2)}) collective-permute-start(bf16[2,192,128]{2,1,0:T(8,128)(2,1)S(1)} %get-tuple-element.71), channel_id=1, source_target_pairs={{0,255},{1,240},{2,241},{3,242},{4,243},{5,244},{6,245},{7,246},{8... | collective-permute-start | bytes 294920 | tf_op jit(solution)/shard_map/ppermute | solution.py:409
  20.6 1.2 collective-permute-start.1
  21.8 0.8 collective-permute-start.9
  22.5 0.3 collective-permute-start.10
  22.9 0.0 collective-permute-done.5.q10_ref
  22.9 4.6 %collective-permute-start.11 = (bf16[2,192,128]{2,1,0:T(8,128)(2,1)S(1)}, bf16[2,192,128]{2,1,0:T(8,128)(2,1)S(1)}, u32[]{:S(2)}, u32[]{:S(2)}) collective-permute-start(bf16[2,192,128]{2,1,0:T(8,128)(2,1)S(1)} %get-tuple-element.95), channel_id=1, source_target_pairs={{0,15},{1,0},{2,1},{3,2},{4,3},{5,4},{6,5},{7,6},{8,7},{9,8},{10,9... | collective-permute-start | bytes 294920 | tf_op jit(solution)/shard_map/ppermute | solution.py:409
  27.5 0.9 copy-done.3
  28.4 0.1 copy-done.5
  28.5 16.8 %attend.3 = (bf16[2,192,128]{2,1,0:T(8,128)(2,1)S(1)}, bf16[2,192,128]{2,1,0:T(8,128)(2,1)S(1)}, bf16[2,192,128]{2,1,0:T(8,128)(2,1)S(1)}, bf16[2,192,128]{2,1,0:T(8,128)(2,1)S(1)}, f32[1280,128]{1,0:T(8,128)S(1)}) custom-call(bf16[2,192,128]{2,1,0:T(8,128)(2,1)S(1)} %collective-permute-done.3.q00_ref, ...), custom_call_target="tpu_custom_call" | custom-call | flops 9663676416 | bytes 4194304 | tf_op jit(solution)/shard_map/attend/pallas_call | solution.py:373
  45.3 0.0 collective-permute-done.q00_ref
  45.3 0.1 collective-permute-start.2
  45.4 0.0 collective-permute-done.9.q00_ref
  45.4 3.1 %collective-permute-start.6 = (bf16[2,192,128]{2,1,0:T(8,128)(2,1)S(1)}, bf16[2,192,128]{2,1,0:T(8,128)(2,1)S(1)}, u32[]{:S(2)}, u32[]{:S(2)}) collective-permute-start(bf16[2,192,128]{2,1,0:T(8,128)(2,1)S(1)} %get-tuple-element.85), channel_id=1, source_target_pairs={{0,17},{1,18},{2,19},{3,20},{4,21},{5,22},{6,23},{7,24},{8,25},{9,... | collective-permute-start | bytes 294920 | tf_op jit(solution)/shard_map/ppermute | solution.py:409
  48.4 0.0 collective-permute-done.10.q01_ref
  48.4 0.6 collective-permute-start.8
  49.1 11.7 %attend.4 = (bf16[2,192,128]{2,1,0:T(8,128)(2,1)S(1)}, bf16[2,192,128]{2,1,0:T(8,128)(2,1)S(1)}, bf16[2,192,128]{2,1,0:T(8,128)(2,1)S(1)}, bf16[2,192,128]{2,1,0:T(8,128)(2,1)S(1)}, f32[1280,128]{1,0:T(8,128)S(1)}) custom-call(bf16[2,192,128]{2,1,0:T(8,128)(2,1)S(1)} %collective-permute-done.9.q00_ref, ...), custom_call_target="tpu_custom_call" | custom-call | flops 9663676416 | bytes 4194304 | tf_op jit(solution)/shard_map/attend/pallas_call | solution.py:373
  60.8 0.1 collective-permute-start.12
  60.9 0.0 collective-permute-done.2.q10_ref
  60.9 0.3 collective-permute-start.13
  61.2 0.0 collective-permute-done.6.refs_0_
  61.2 5.0 %collective-permute-start.14 = (bf16[2,192,128]{2,1,0:T(8,128)(2,1)S(1)}, bf16[2,192,128]{2,1,0:T(8,128)(2,1)S(1)}, u32[]{:S(2)}, u32[]{:S(2)}) collective-permute-start(bf16[2,192,128]{2,1,0:T(8,128)(2,1)S(1)} %get-tuple-element.102), channel_id=1, source_target_pairs={{0,1},{1,2},{2,3},{3,4},{4,5},{5,6},{6,7},{7,8},{8,9},{9,10},{10,1... | collective-permute-start | bytes 294920 | tf_op jit(solution)/shard_map/ppermute | solution.py:409
  66.2 0.0 collective-permute-done.7.refs_1_
  66.2 0.0 collective-permute-done.8.refs_2_
  66.2 7.2 %attend.5 = (bf16[2,192,128]{2,1,0:T(8,128)(2,1)S(1)}, bf16[2,192,128]{2,1,0:T(8,128)(2,1)S(1)}, bf16[2,192,128]{2,1,0:T(8,128)(2,1)S(1)}, bf16[2,192,128]{2,1,0:T(8,128)(2,1)S(1)}, bf16[1280,128]{1,0:T(8,128)(2,1)}) custom-call(bf16[2,192,128]{2,1,0:T(8,128)(2,1)S(1)} %collective-permute-done.q00_ref, ...), custom_call_target="tpu_custom_call" | custom-call | flops 9663676416 | bytes 4194304 | tf_op jit(solution)/shard_map/attend/pallas_call | solution.py:373
  73.5 6.4 %all-to-all-start = ((bf16[32,40,128]{2,1,0:T(8,128)(2,1)}), bf16[32,40,128]{2,1,0:T(8,128)(2,1)S(1)}, u32[]{:S(2)}, u32[]{:S(2)}) async-start(bf16[32,40,128]{2,1,0:T(8,128)(2,1)} %bitcast.2), calls=%async_computation | async-start | bytes 655360 | tf_op jit(solution)/shard_map/all_to_all | solution.py:419
  79.9 2.6 %collective-permute-start.15 = (bf16[2,192,128]{2,1,0:T(8,128)(2,1)S(1)}, bf16[2,192,128]{2,1,0:T(8,128)(2,1)S(1)}, u32[]{:S(2)}, u32[]{:S(2)}) collective-permute-start(bf16[2,192,128]{2,1,0:T(8,128)(2,1)S(1)} %get-tuple-element.113), channel_id=1, source_target_pairs={{0,17},{1,18},{2,19},{3,20},{4,21},{5,22},{6,23},{7,24},{8,25},{9,... | collective-permute-start | bytes 294920 | tf_op jit(solution)/shard_map/ppermute | solution.py:409
  82.5 2.7 %collective-permute-start.16 = (bf16[2,192,128]{2,1,0:T(8,128)(2,1)S(1)}, bf16[2,192,128]{2,1,0:T(8,128)(2,1)S(1)}, u32[]{:S(2)}, u32[]{:S(2)}) collective-permute-start(bf16[2,192,128]{2,1,0:T(8,128)(2,1)S(1)} %get-tuple-element.114), channel_id=1, source_target_pairs={{0,16},{1,17},{2,18},{3,19},{4,20},{5,21},{6,22},{7,23},{8,24},{9,... | collective-permute-start | bytes 294920 | tf_op jit(solution)/shard_map/ppermute | solution.py:409
  85.2 0.6 collective-permute-start.17
  85.8 6.7 %collective-permute-done.15.refs_8_ = bf16[2,192,128]{2,1,0:T(8,128)(2,1)S(1)} collective-permute-done((bf16[2,192,128]{2,1,0:T(8,128)(2,1)S(1)}, bf16[2,192,128]{2,1,0:T(8,128)(2,1)S(1)}, u32[]{:S(2)}, u32[]{:S(2)}) %collective-permute-start.15) | collective-permute-done | bytes 98336 | tf_op jit(solution)/shard_map/ppermute | solution.py:409
  92.5 1.2 collective-permute-done.16.refs_9_
  93.7 0.1 reduce_sum.24
  93.8 16.3 %all_to_all.15 = bf16[8,40,128]{2,1,0:T(8,128)(2,1)S(1)} all-to-all(bf16[8,40,128]{2,1,0:T(8,128)(2,1)S(1)} %broadcast_in_dim.24), channel_id=1, replica_groups={{0,32,64,96,128,160,192,224},{1,33,65,97,129,161,193,225},{2,34,66,98,1..., dimensions={0} | all-to-all | bytes 163840 | tf_op jit(solution)/shard_map/all_to_all | solution.py:419
  110.1 0.8 broadcast_in_dim.25
  110.9 6.3 %all-to-all-start.2 = ((bf16[32,40,128]{2,1,0:T(8,128)(2,1)}), bf16[32,40,128]{2,1,0:T(8,128)(2,1)S(1)}, u32[]{:S(2)}, u32[]{:S(2)}) async-start(bf16[32,40,128]{2,1,0:T(8,128)(2,1)} %broadcast_in_dim.25), calls=%async_computation.2 | async-start | bytes 655360 | tf_op jit(solution)/shard_map/all_to_all | solution.py:419
  117.2 1.6 %unpack.1 = (bf16[8,8,24,192]{3,2,1,0:T(8,128)(2,1)}, bf16[8,8,24,192]{3,2,1,0:T(8,128)(2,1)}) custom-call(bf16[2,192,128]{2,1,0:T(8,128)(2,1)S(1)} %collective-permute-done.6.refs_0_, bf16[2,192,128]{2,1,0:T(8,128)(2,1)S(1)} %collective-permute-done.7.refs_1_, bf16[2,192,128]{2,1,0:T(8,128)(2,1)S(1)} %collective-permute-done.8.refs_2_, ...), custom_call_target="tpu_custom_call" | custom-call | tf_op jit(solution)/shard_map/unpack/pallas_call | solution.py:122
  118.8 8.2 %all-to-all-done.2 = bf16[32,40,128]{2,1,0:T(8,128)(2,1)S(1)} async-done(((bf16[32,40,128]{2,1,0:T(8,128)(2,1)}), bf16[32,40,128]{2,1,0:T(8,128)(2,1)S(1)}, u32[]{:S(2)}, u32[]{:S(2)}) %all-to-all-start.2) | async-done | bytes 327712 | tf_op jit(solution)/shard_map/all_to_all | solution.py:419
  127.0 0.7 copy-done.8
  127.7 1.9 %unpack_grads.1 = (f32[192,576]{1,0:T(8,128)}, f32[192,192]{1,0:T(8,128)}, f32[1,192]{1,0:T(1,128)}, f32[1,192]{1,0:T(1,128)}) custom-call(bf16[1280,128]{1,0:T(8,128)(2,1)} %bitcast.8), custom_call_target="tpu_custom_call" | custom-call | tf_op jit(solution)/shard_map/unpack_grads/pallas_call | solution.py:449
  (22 shorter events, 0.1 us)
Async XLA Ops:
  0.6 0.7 copy-start.7
  0.6 0.7 copy-start.6
  1.3 1.1 copy-start
  2.5 1.1 copy-start.1
  3.6 0.9 copy-start.2
  4.5 0.9 copy-start.4
  6.2 15.6 %collective-permute-start.3 = (bf16[2,192,128]{2,1,0:T(8,128)(2,1)S(1)}, bf16[2,192,128]{2,1,0:T(8,128)(2,1)S(1)}, u32[]{:S(2)}, u32[]{:S(2)}) collective-permute-start(bf16[2,192,128]{2,1,0:T(8,128)(2,1)S(1)} %get-tuple-element.75), channel_id=1, source_target_pairs={{0,255},{1,240},{2,241},{3,242},{4,243},{5,244},{6,245},{7,246},{8... | collective-permute-start | bytes 294920 | tf_op jit(solution)/shard_map/ppermute | solution.py:409
  14.1 8.4 %collective-permute-start.4 = (bf16[2,192,128]{2,1,0:T(8,128)(2,1)S(1)}, bf16[2,192,128]{2,1,0:T(8,128)(2,1)S(1)}, u32[]{:S(2)}, u32[]{:S(2)}) collective-permute-start(bf16[2,192,128]{2,1,0:T(8,128)(2,1)S(1)} %get-tuple-element.76), channel_id=1, source_target_pairs={{0,240},{1,241},{2,242},{3,243},{4,244},{5,245},{6,246},{7,247},{8... | collective-permute-start | bytes 294920 | tf_op jit(solution)/shard_map/ppermute | solution.py:409
  14.4 8.5 %collective-permute-start.5 = (bf16[2,192,128]{2,1,0:T(8,128)(2,1)S(1)}, bf16[2,192,128]{2,1,0:T(8,128)(2,1)S(1)}, u32[]{:S(2)}, u32[]{:S(2)}) collective-permute-start(bf16[2,192,128]{2,1,0:T(8,128)(2,1)S(1)} %get-tuple-element.77), channel_id=1, source_target_pairs={{0,15},{1,0},{2,1},{3,2},{4,3},{5,4},{6,5},{7,6},{8,7},{9,8},{10,9... | collective-permute-start | bytes 294920 | tf_op jit(solution)/shard_map/ppermute | solution.py:409
  17.9 27.3 %collective-permute-start = (bf16[2,192,128]{2,1,0:T(8,128)(2,1)S(1)}, bf16[2,192,128]{2,1,0:T(8,128)(2,1)S(1)}, u32[]{:S(2)}, u32[]{:S(2)}) collective-permute-start(bf16[2,192,128]{2,1,0:T(8,128)(2,1)S(1)} %get-tuple-element.71), channel_id=1, source_target_pairs={{0,255},{1,240},{2,241},{3,242},{4,243},{5,244},{6,245},{7,246},{8... | collective-permute-start | bytes 294920 | tf_op jit(solution)/shard_map/ppermute | solution.py:409
  20.6 40.2 %collective-permute-start.1 = (bf16[2,192,128]{2,1,0:T(8,128)(2,1)S(1)}, bf16[2,192,128]{2,1,0:T(8,128)(2,1)S(1)}, u32[]{:S(2)}, u32[]{:S(2)}) collective-permute-start(bf16[2,192,128]{2,1,0:T(8,128)(2,1)S(1)} %get-tuple-element.72), channel_id=1, source_target_pairs={{0,240},{1,241},{2,242},{3,243},{4,244},{5,245},{6,246},{7,247},{8... | collective-permute-start | bytes 294920 | tf_op jit(solution)/shard_map/ppermute | solution.py:409
  21.8 23.6 %collective-permute-start.9 = (bf16[2,192,128]{2,1,0:T(8,128)(2,1)S(1)}, bf16[2,192,128]{2,1,0:T(8,128)(2,1)S(1)}, u32[]{:S(2)}, u32[]{:S(2)}) collective-permute-start(bf16[2,192,128]{2,1,0:T(8,128)(2,1)S(1)} %get-tuple-element.93), channel_id=1, source_target_pairs={{0,255},{1,240},{2,241},{3,242},{4,243},{5,244},{6,245},{7,246},{8... | collective-permute-start | bytes 294920 | tf_op jit(solution)/shard_map/ppermute | solution.py:409
  22.5 25.9 %collective-permute-start.10 = (bf16[2,192,128]{2,1,0:T(8,128)(2,1)S(1)}, bf16[2,192,128]{2,1,0:T(8,128)(2,1)S(1)}, u32[]{:S(2)}, u32[]{:S(2)}) collective-permute-start(bf16[2,192,128]{2,1,0:T(8,128)(2,1)S(1)} %get-tuple-element.94), channel_id=1, source_target_pairs={{0,240},{1,241},{2,242},{3,243},{4,244},{5,245},{6,246},{7,247},{8... | collective-permute-start | bytes 294920 | tf_op jit(solution)/shard_map/ppermute | solution.py:409
  22.9 25.6 %collective-permute-start.11 = (bf16[2,192,128]{2,1,0:T(8,128)(2,1)S(1)}, bf16[2,192,128]{2,1,0:T(8,128)(2,1)S(1)}, u32[]{:S(2)}, u32[]{:S(2)}) collective-permute-start(bf16[2,192,128]{2,1,0:T(8,128)(2,1)S(1)} %get-tuple-element.95), channel_id=1, source_target_pairs={{0,15},{1,0},{2,1},{3,2},{4,3},{5,4},{6,5},{7,6},{8,7},{9,8},{10,9... | collective-permute-start | bytes 294920 | tf_op jit(solution)/shard_map/ppermute | solution.py:409
  27.5 0.9 copy-start.3
  27.5 1.0 copy-start.5
  45.3 15.6 %collective-permute-start.2 = (bf16[2,192,128]{2,1,0:T(8,128)(2,1)S(1)}, bf16[2,192,128]{2,1,0:T(8,128)(2,1)S(1)}, u32[]{:S(2)}, u32[]{:S(2)}) collective-permute-start(bf16[2,192,128]{2,1,0:T(8,128)(2,1)S(1)} %get-tuple-element.73), channel_id=1, source_target_pairs={{0,15},{1,0},{2,1},{3,2},{4,3},{5,4},{6,5},{7,6},{8,7},{9,8},{10,9... | collective-permute-start | bytes 294920 | tf_op jit(solution)/shard_map/ppermute | solution.py:409
  45.4 15.8 %collective-permute-start.6 = (bf16[2,192,128]{2,1,0:T(8,128)(2,1)S(1)}, bf16[2,192,128]{2,1,0:T(8,128)(2,1)S(1)}, u32[]{:S(2)}, u32[]{:S(2)}) collective-permute-start(bf16[2,192,128]{2,1,0:T(8,128)(2,1)S(1)} %get-tuple-element.85), channel_id=1, source_target_pairs={{0,17},{1,18},{2,19},{3,20},{4,21},{5,22},{6,23},{7,24},{8,25},{9,... | collective-permute-start | bytes 294920 | tf_op jit(solution)/shard_map/ppermute | solution.py:409
  48.4 17.8 %collective-permute-start.7 = (bf16[2,192,128]{2,1,0:T(8,128)(2,1)S(1)}, bf16[2,192,128]{2,1,0:T(8,128)(2,1)S(1)}, u32[]{:S(2)}, u32[]{:S(2)}) collective-permute-start(bf16[2,192,128]{2,1,0:T(8,128)(2,1)S(1)} %get-tuple-element.86), channel_id=1, source_target_pairs={{0,16},{1,17},{2,18},{3,19},{4,20},{5,21},{6,22},{7,23},{8,24},{9,... | collective-permute-start | bytes 294920 | tf_op jit(solution)/shard_map/ppermute | solution.py:409
  48.4 17.8 %collective-permute-start.8 = (bf16[2,192,128]{2,1,0:T(8,128)(2,1)S(1)}, bf16[2,192,128]{2,1,0:T(8,128)(2,1)S(1)}, u32[]{:S(2)}, u32[]{:S(2)}) collective-permute-start(bf16[2,192,128]{2,1,0:T(8,128)(2,1)S(1)} %get-tuple-element.87), channel_id=1, source_target_pairs={{0,1},{1,2},{2,3},{3,4},{4,5},{5,6},{6,7},{7,8},{8,9},{9,10},{10,1... | collective-permute-start | bytes 294920 | tf_op jit(solution)/shard_map/ppermute | solution.py:409
  60.8 12.7 %collective-permute-start.12 = (bf16[2,192,128]{2,1,0:T(8,128)(2,1)S(1)}, bf16[2,192,128]{2,1,0:T(8,128)(2,1)S(1)}, u32[]{:S(2)}, u32[]{:S(2)}) collective-permute-start(bf16[2,192,128]{2,1,0:T(8,128)(2,1)S(1)} %get-tuple-element.100), channel_id=1, source_target_pairs={{0,17},{1,18},{2,19},{3,20},{4,21},{5,22},{6,23},{7,24},{8,25},{9,... | collective-permute-start | bytes 294920 | tf_op jit(solution)/shard_map/ppermute | solution.py:409
  60.9 12.6 %collective-permute-start.13 = (bf16[2,192,128]{2,1,0:T(8,128)(2,1)S(1)}, bf16[2,192,128]{2,1,0:T(8,128)(2,1)S(1)}, u32[]{:S(2)}, u32[]{:S(2)}) collective-permute-start(bf16[2,192,128]{2,1,0:T(8,128)(2,1)S(1)} %get-tuple-element.101), channel_id=1, source_target_pairs={{0,16},{1,17},{2,18},{3,19},{4,20},{5,21},{6,22},{7,23},{8,24},{9,... | collective-permute-start | bytes 294920 | tf_op jit(solution)/shard_map/ppermute | solution.py:409
  61.2 12.2 %collective-permute-start.14 = (bf16[2,192,128]{2,1,0:T(8,128)(2,1)S(1)}, bf16[2,192,128]{2,1,0:T(8,128)(2,1)S(1)}, u32[]{:S(2)}, u32[]{:S(2)}) collective-permute-start(bf16[2,192,128]{2,1,0:T(8,128)(2,1)S(1)} %get-tuple-element.102), channel_id=1, source_target_pairs={{0,1},{1,2},{2,3},{3,4},{4,5},{5,6},{6,7},{7,8},{8,9},{9,10},{10,1... | collective-permute-start | bytes 294920 | tf_op jit(solution)/shard_map/ppermute | solution.py:409
  73.5 20.2 %all-to-all-start = ((bf16[32,40,128]{2,1,0:T(8,128)(2,1)}), bf16[32,40,128]{2,1,0:T(8,128)(2,1)S(1)}, u32[]{:S(2)}, u32[]{:S(2)}) async-start(bf16[32,40,128]{2,1,0:T(8,128)(2,1)} %bitcast.2), calls=%async_computation | async-start | bytes 655360 | tf_op jit(solution)/shard_map/all_to_all | solution.py:419
  79.9 12.7 %collective-permute-start.15 = (bf16[2,192,128]{2,1,0:T(8,128)(2,1)S(1)}, bf16[2,192,128]{2,1,0:T(8,128)(2,1)S(1)}, u32[]{:S(2)}, u32[]{:S(2)}) collective-permute-start(bf16[2,192,128]{2,1,0:T(8,128)(2,1)S(1)} %get-tuple-element.113), channel_id=1, source_target_pairs={{0,17},{1,18},{2,19},{3,20},{4,21},{5,22},{6,23},{7,24},{8,25},{9,... | collective-permute-start | bytes 294920 | tf_op jit(solution)/shard_map/ppermute | solution.py:409
  82.5 11.2 %collective-permute-start.16 = (bf16[2,192,128]{2,1,0:T(8,128)(2,1)S(1)}, bf16[2,192,128]{2,1,0:T(8,128)(2,1)S(1)}, u32[]{:S(2)}, u32[]{:S(2)}) collective-permute-start(bf16[2,192,128]{2,1,0:T(8,128)(2,1)S(1)} %get-tuple-element.114), channel_id=1, source_target_pairs={{0,16},{1,17},{2,18},{3,19},{4,20},{5,21},{6,22},{7,23},{8,24},{9,... | collective-permute-start | bytes 294920 | tf_op jit(solution)/shard_map/ppermute | solution.py:409
  85.2 8.5 %collective-permute-start.17 = (bf16[2,192,128]{2,1,0:T(8,128)(2,1)S(1)}, bf16[2,192,128]{2,1,0:T(8,128)(2,1)S(1)}, u32[]{:S(2)}, u32[]{:S(2)}) collective-permute-start(bf16[2,192,128]{2,1,0:T(8,128)(2,1)S(1)} %get-tuple-element.115), channel_id=1, source_target_pairs={{0,1},{1,2},{2,3},{3,4},{4,5},{5,6},{6,7},{7,8},{8,9},{9,10},{10,1... | collective-permute-start | bytes 294920 | tf_op jit(solution)/shard_map/ppermute | solution.py:409
  110.9 16.1 %all-to-all-start.2 = ((bf16[32,40,128]{2,1,0:T(8,128)(2,1)}), bf16[32,40,128]{2,1,0:T(8,128)(2,1)S(1)}, u32[]{:S(2)}, u32[]{:S(2)}) async-start(bf16[32,40,128]{2,1,0:T(8,128)(2,1)} %broadcast_in_dim.25), calls=%async_computation.2 | async-start | bytes 655360 | tf_op jit(solution)/shard_map/all_to_all | solution.py:419
  127.0 0.7 copy-start.8
